TPU v7x, 256 devices: a whole 4x4x8 slice. The times are simulated.
256 devices in a mesh: seq: 64 (over z, x, core), head: 4 (over y).
Axes of the slice: x: 4, y: 4, z: 8, core: 2. Of those that a mesh axis runs over, the one named last changes fastest.
Arguments:
- query_key: bfloat16 [32768, 128], P('seq'), may hold values from -1.5 to 1.5
- values: bfloat16 [32768, 5120], P('seq', 'head'), may hold values from -0.119628906 to 0.119628906
- cotangent: bfloat16 [32768, 5120], P('seq', 'head'), may hold values from -0.119628906 to 0.119628906
- level_gain: float32 [16, 15, 80], P(None, None, 'head'), may hold values from 0.1 to 1
- level_code: int32 [512], P('seq'), may hold values from 0 to 15
Outputs:
- mixed: bfloat16 [32768, 5120], P('seq', 'head')
- grad_qk: float32 [32768, 128], P('seq')
- grad_values: bfloat16 [32768, 5120], P('seq', 'head')
Inputs may be any that keep to these rules, and one draw needn't show every extreme that they name: `level_code`: each span's row of the weight table.
All inputs are finite; a program needn't handle non-finite values.
Results may differ from a plain program's by a relative error of at most 0.005.
Values sent between devices are 32-bit elements; how exact they have to be, the bound alone decides.
No kernel may reach another device: no remote copies, remote signals or barrier semaphores. Data moves between devices by JAX's collectives and lax.ppermute only.
A program may use at most 128 MiB of HBM per device.

v0:
```python
import jax
import jax.numpy as jnp
from jax import lax
from jax.sharding import PartitionSpec as P

HEAD_DIM = 64
CH = 64
precise = lax.Precision.HIGHEST


def partner_2(value, axis, bit):
    mask = 2**bit
    pairs = [(source, source ^ mask) for source in range(lax.axis_size(axis))]
    return lax.ppermute(value, axis, pairs)


def bit_length(numbers, top_bits):
    bit_total = jnp.zeros_like(numbers)
    for bit_power in range(top_bits):
        bit_total = bit_total + (numbers >= 1 << bit_power).astype(jnp.int32)
    return bit_total


def local_levels(span_count):
    span_ids = jnp.arange(span_count, dtype=jnp.int32)
    return bit_length(span_ids[:, None] ^ span_ids[None, :], 8)


def local(query_key, values, cotangent, level_gain, level_code):
    tok_rows, state_dim = query_key.shape
    head_cols = values.shape[1]
    codes, levels, group_heads = level_gain.shape
    span_count = tok_rows // CH
    span_levels = span_count.bit_length() - 1
    seq_levels = lax.axis_size("seq").bit_length() - 1
    position = lax.axis_index("seq")
    picked = (level_code[:, None] == jnp.arange(codes, dtype=jnp.int32)[None, :]).astype(
        jnp.float32
    )
    level_weight = jnp.dot(
        picked, level_gain.reshape(codes, levels * group_heads), precision=precise
    ).reshape(span_count, levels, group_heads)
    cross_cols = jnp.repeat(
        level_weight[:, span_levels + 1 : span_levels + 1 + seq_levels, :], HEAD_DIM, axis=-1
    )
    own_state = lax.dot_general(
        query_key, values, (((0,), (0,)), ((), ())), preferred_element_type=jnp.float32
    )
    q_spans = query_key.reshape(span_count, CH, state_dim)
    c_spans = cotangent.reshape(span_count, CH, head_cols)
    span_grad = jnp.einsum("cti,ctj->cij", q_spans, c_spans, preferred_element_type=jnp.float32)
    level_grad = jnp.einsum("cij,clj->lij", span_grad, cross_cols, precision=precise)
    siblings = []
    adjoint = jnp.zeros_like(own_state)
    block_sum = own_state
    level_carry = level_grad
    for level_bit in range(seq_levels):
        partner = partner_2(block_sum, "seq", level_bit)
        upper_half = position >> level_bit & 1 == 1
        siblings.append(jnp.where(upper_half, partner, 0.0))
        block_sum = block_sum + partner
    for level_bit in range(seq_levels):
        partner_grad = partner_2(level_carry, "seq", level_bit)
        upper_half = position >> level_bit & 1 == 1
        adjoint = adjoint + jnp.where(upper_half, 0.0, partner_grad[0])
        level_carry = (level_carry + partner_grad)[1:]
    sibling = jnp.stack(siblings)
    span_state = jnp.einsum("clj,lij->cij", cross_cols, sibling, precision=precise).astype(
        jnp.bfloat16
    )
    adjoint_bf = adjoint.astype(jnp.bfloat16)
    scores = lax.dot_general(
        query_key, query_key, (((1,), (1,)), ((), ())), preferred_element_type=jnp.float32
    )
    onehot = (
        local_levels(span_count)[:, :, None]
        == jnp.arange(span_levels + 1, dtype=jnp.int32)[None, None, :]
    ).astype(jnp.float32)
    local_weight = jnp.einsum(
        "abk,akg->gab", onehot, level_weight[:, : span_levels + 1, :], precision=precise
    )
    causal = jnp.tril(jnp.ones((tok_rows, tok_rows), dtype=bool))
    pair_cols = 2 * HEAD_DIM

    def head_pair(pair_index, running):
        inner_out, dv_inner, d_score = running
        col_start = pair_index * pair_cols
        val_pair = lax.dynamic_slice_in_dim(values, col_start, pair_cols, 1).reshape(
            tok_rows, 2, HEAD_DIM
        )
        cot_pair = lax.dynamic_slice_in_dim(cotangent, col_start, pair_cols, 1).reshape(
            tok_rows, 2, HEAD_DIM
        )
        pair_weight = lax.dynamic_slice_in_dim(local_weight, pair_index * 2, 2, 0)
        weight = jnp.broadcast_to(
            pair_weight[:, :, None, :, None], (2, span_count, CH, span_count, CH)
        ).reshape(2, tok_rows, tok_rows)
        mixing = jnp.where(causal, weight * scores, 0.0).astype(jnp.bfloat16)
        part_out = jnp.einsum(
            "gts,sgp->tgp", mixing, val_pair, preferred_element_type=jnp.float32
        ).reshape(tok_rows, pair_cols)
        d_mix = jnp.einsum("tgp,sgp->gts", cot_pair, val_pair, preferred_element_type=jnp.float32)
        d_score = d_score + jnp.sum(jnp.where(causal, weight * d_mix, 0.0), axis=0)
        part_dv = jnp.einsum(
            "gts,tgp->sgp", mixing, cot_pair, preferred_element_type=jnp.float32
        ).reshape(tok_rows, pair_cols)
        inner_out = lax.dynamic_update_slice_in_dim(inner_out, part_out, col_start, 1)
        dv_inner = lax.dynamic_update_slice_in_dim(dv_inner, part_dv, col_start, 1)
        return (inner_out, dv_inner, d_score)

    start_state = (
        jnp.zeros((tok_rows, head_cols), jnp.float32),
        jnp.zeros((tok_rows, head_cols), jnp.float32),
        jnp.zeros((tok_rows, tok_rows), jnp.float32),
    )
    inner_out, dv_inner, d_score = lax.fori_loop(0, group_heads // 2, head_pair, start_state)
    outer_out = jnp.einsum(
        "cti,cij->ctj", q_spans, span_state, preferred_element_type=jnp.float32
    ).reshape(tok_rows, head_cols)
    mixed = (inner_out + outer_out).astype(jnp.bfloat16)
    dq_outer = jnp.einsum(
        "ctj,cij->cti", c_spans, span_state, preferred_element_type=jnp.float32
    ).reshape(tok_rows, state_dim)
    dv_outer = jnp.dot(query_key, adjoint_bf, preferred_element_type=jnp.float32)
    dk_outer = lax.dot_general(
        values, adjoint_bf, (((1,), (1,)), ((), ())), preferred_element_type=jnp.float32
    )
    q_float = query_key.astype(jnp.float32)
    dq_inner = jnp.dot(d_score, q_float, precision=precise) + lax.dot_general(
        d_score, q_float, (((0,), (0,)), ((), ())), precision=precise
    )
    head_part = dq_inner + dq_outer + dk_outer
    grad_qk = lax.psum(head_part, "head")
    grad_values = (dv_inner + dv_outer).astype(jnp.bfloat16)
    return (mixed, grad_qk, grad_values)


def solution(mesh):
    placed = (P("seq", None), P("seq", "head"), P("seq", "head"), P(None, None, "head"), P("seq"))
    return jax.shard_map(
        local,
        mesh=mesh,
        in_specs=placed,
        out_specs=(P("seq", "head"), P("seq", None), P("seq", "head")),
        check_vma=False,
    )
```

profile of v0, /device:TPU:2, one launch (start us, length us, event | category | flops | bytes accessed | tf_op | source)
XLA Modules:
  0.0 713.1 jit_solution(9387156875039487626)
XLA Ops:
  8.1 4.5 fusion.36
  12.6 6.3 copy.78
  19.9 2.7 copy-done.2
  24.0 10.4 %fusion.37 = f32[1280,6,128]{2,1,0:T(8,128)} fusion(f32[8,6,1280]{0,1,2:T(8,128)S(1)} %bitcast.108, f32[8,128,1280]{1,0,2:T(8,128)S(1)} %copy-done.4), kind=kOutput, calls=%fused_computation.70 | convolution fusion | flops 94371840 | bytes 9420800 | tf_op jit(solution)/shard_map/cij,clj->lij/dot_general | solution.py:52
  34.4 5.7 copy.79
  40.0 7.0 collective-permute-done.6
  47.0 3.8 slice_add_fusion
  53.2 71.2 %collective-permute-done.7 = f32[5,128,1280]{2,1,0:T(8,128)S(1)} collective-permute-done((f32[5,128,1280]{2,1,0:T(8,128)S(1)}, f32[5,128,1280]{2,1,0:T(8,128)S(1)}, u32[]{:S(2)}, u32[]{:S(2)}) %collective-permute-start.7) | collective-permute-done | bytes 3276832 | tf_op jit(solution)/shard_map/ppermute | solution.py:14
  135.8 64.5 %collective-permute-done.1 = f32[128,1280]{1,0:T(8,128)S(1)} collective-permute-done((f32[128,1280]{1,0:T(8,128)S(1)}, f32[128,1280]{1,0:T(8,128)S(1)}, u32[]{:S(2)}, u32[]{:S(2)}) %collective-permute-start.1) | collective-permute-done | bytes 655392 | tf_op jit(solution)/shard_map/ppermute | solution.py:14
  202.9 3.7 slice_add_fusion.2
  210.4 230.9 %while.19 = (s32[]{:T(128)}, f32[512,1280]{1,0:T(8,128)}, f32[512,1280]{0,1:T(8,128)}, f32[512,512]{1,0:T(8,128)}, bf16[512,1280]{1,0:T(8,128)(2,1)S(1)}, /*inde...) while((s32[]{:T(128)}, f32[512,1280]{1,0:T(8,128)}, ...), condition=%wide.region_2.3_spmd.clone.clone, body=%wide.region_0.2_spmd.clone.clone.sunk | while | flops 204996608 | bytes 29099832 | solution.py:116
  215.8 3.4 reshape.141
  238.0 3.4 reshape.141
  261.2 3.4 reshape.141
  284.4 3.4 reshape.141
  307.6 3.4 reshape.141
  330.8 3.4 reshape.141
  354.0 3.4 reshape.141
  377.1 3.4 reshape.141
  400.3 3.4 reshape.141
  423.5 3.4 reshape.141
  450.9 21.2 %collective-permute-done.3 = f32[128,1280]{1,0:T(8,128)S(1)} collective-permute-done((f32[128,1280]{1,0:T(8,128)S(1)}, f32[128,1280]{1,0:T(8,128)S(1)}, u32[]{:S(2)}, u32[]{:S(2)}) %collective-permute-start.3) | collective-permute-done | bytes 655392 | tf_op jit(solution)/shard_map/ppermute | solution.py:14
  474.1 59.5 %collective-permute-done.4 = f32[128,1280]{1,0:T(8,128)S(1)} collective-permute-done((f32[128,1280]{1,0:T(8,128)S(1)}, f32[128,1280]{1,0:T(8,128)S(1)}, u32[]{:S(2)}, u32[]{:S(2)}) %collective-permute-start.4) | collective-permute-done | bytes 655392 | tf_op jit(solution)/shard_map/ppermute | solution.py:14
  533.7 6.0 collective-permute-start.5
  541.9 34.5 %collective-permute-done.5 = f32[128,1280]{1,0:T(8,128)S(1)} collective-permute-done((f32[128,1280]{1,0:T(8,128)S(1)}, f32[128,1280]{1,0:T(8,128)S(1)}, u32[]{:S(2)}, u32[]{:S(2)}) %collective-permute-start.5) | collective-permute-done | bytes 655392 | tf_op jit(solution)/shard_map/ppermute | solution.py:14
  576.5 17.7 %collective-permute-done.11 = f32[1,128,1280]{2,1,0:T(8,128)S(1)} collective-permute-done((f32[1,128,1280]{2,1,0:T(8,128)S(1)}, f32[1,128,1280]{2,1,0:T(8,128)S(1)}, u32[]{:S(2)}, u32[]{:S(2)}) %collective-permute-start.11) | collective-permute-done | bytes 655392 | tf_op jit(solution)/shard_map/ppermute | solution.py:14
  594.2 3.0 fusion.9
  597.2 5.7 copy.73
  602.9 13.7 %convert_bitcast_fusion = bf16[8,128,1280]{1,0,2:T(8,128)(2,1)} fusion(f32[6,128,1280]{1,0,2:T(8,128)} %copy.73, f32[8,6,1280]{0,1,2:T(8,128)} %bitcast.109), kind=kOutput, calls=%fused_computation.17 | convolution fusion | flops 95682560 | bytes 6799360 | tf_op jit(solution)/shard_map/clj,lij->cij/dot_general | solution.py:68
  616.6 3.8 copy.75
  627.0 3.2 fusion.4
  632.3 72.3 %all-reduce.2.cloned.1.call-done = f32[512,128]{1,0:T(8,128)} async-done(((f32[512,128]{1,0:T(8,128)}), f32[512,128]{1,0:T(8,128)}) %all-reduce.2.cloned.1.call-update) | async-done | bytes 262160 | tf_op jit(solution)/shard_map/psum | solution.py:133
  (266 shorter events, 243.4 us)
Async XLA Ops:
  7.2 697.4 %all-reduce.2.cloned.1.call-start = ((), (), s32[]{:S(2)}) async-start(), calls=%async_computation | async-start | bytes 524288 | tf_op jit(solution)/shard_map/psum | solution.py:133
  12.6 6.3 copy-start.16
  12.6 6.6 copy-start.17
  19.6 4.4 copy-start.4
  19.9 2.7 copy-start.2
  40.0 7.0 collective-permute-start.6
  47.0 3.8 copy-start.10
  50.8 77.7 %copy-start.7 = (bf16[512,1280]{1,0:T(8,128)(2,1)S(1)}, bf16[512,1280]{1,0:T(8,128)(2,1)}, u32[]{:S(2)}) copy-start(bf16[512,1280]{1,0:T(8,128)(2,1)} %param.8) | copy-start | bytes 3932164
  50.8 73.6 %collective-permute-start.7 = (f32[5,128,1280]{2,1,0:T(8,128)S(1)}, f32[5,128,1280]{2,1,0:T(8,128)S(1)}, u32[]{:S(2)}, u32[]{:S(2)}) collective-permute-start(f32[5,128,1280]{2,1,0:T(8,128)S(1)} %slice_add_fusion), channel_id=1, source_target_pairs={{0,8},{4,12},{8,0},{12,4},{16,24},{20,28},{24,16},{28,20},{32,40},... | collective-permute-start | bytes 9830408 | tf_op jit(solution)/shard_map/ppermute | solution.py:14
  126.9 76.0 %collective-permute-start.8 = (f32[4,128,1280]{2,1,0:T(8,128)}, f32[4,128,1280]{2,1,0:T(8,128)}, u32[]{:S(2)}, u32[]{:S(2)}) collective-permute-start(f32[4,128,1280]{2,1,0:T(8,128)} %slice_add_fusion.1), channel_id=1, source_target_pairs={{0,16},{4,20},{8,24},{12,28},{16,0},{20,4},{24,8},{28,12},{32,48},... | collective-permute-start | bytes 7864328 | tf_op jit(solution)/shard_map/ppermute | solution.py:14
  128.9 2.2 collective-permute-start
  132.0 68.3 %collective-permute-start.1 = (f32[128,1280]{1,0:T(8,128)S(1)}, f32[128,1280]{1,0:T(8,128)S(1)}, u32[]{:S(2)}, u32[]{:S(2)}) collective-permute-start(f32[128,1280]{1,0:T(8,128)S(1)} %add.163), channel_id=1, source_target_pairs={{0,8},{4,12},{8,0},{12,4},{16,24},{20,28},{24,16},{28,20},{32,40},... | collective-permute-start | bytes 1966088 | tf_op jit(solution)/shard_map/ppermute | solution.py:14
  200.2 6.3 copy-start.12
  201.3 241.8 %collective-permute-start.2 = (f32[128,1280]{1,0:T(8,128)}, f32[128,1280]{1,0:T(8,128)}, u32[]{:S(2)}, u32[]{:S(2)}) collective-permute-start(f32[128,1280]{1,0:T(8,128)} %add.164), channel_id=1, source_target_pairs={{0,16},{4,20},{8,24},{12,28},{16,0},{20,4},{24,8},{28,12},{32,48},... | collective-permute-start | bytes 1966088 | tf_op jit(solution)/shard_map/ppermute | solution.py:14
  206.6 239.8 %collective-permute-start.9 = (f32[3,128,1280]{2,1,0:T(8,128)}, f32[3,128,1280]{2,1,0:T(8,128)}, u32[]{:S(2)}, u32[]{:S(2)}) collective-permute-start(f32[3,128,1280]{2,1,0:T(8,128)} %slice_add_fusion.2), channel_id=1, source_target_pairs={{0,32},{4,36},{8,40},{12,44},{16,48},{20,52},{24,56},{28,60},{32,0... | collective-permute-start | bytes 5898248 | tf_op jit(solution)/shard_map/ppermute | solution.py:14
  253.3 2.5 copy-start.8
  276.4 2.5 copy-start.8
  299.6 2.5 copy-start.8
  322.8 2.5 copy-start.8
  346.0 2.5 copy-start.8
  369.2 2.5 copy-start.8
  392.3 2.5 copy-start.8
  415.5 2.5 copy-start.8
  443.1 6.9 copy-start.15
  444.5 27.6 %collective-permute-start.3 = (f32[128,1280]{1,0:T(8,128)S(1)}, f32[128,1280]{1,0:T(8,128)S(1)}, u32[]{:S(2)}, u32[]{:S(2)}) collective-permute-start(f32[128,1280]{1,0:T(8,128)S(1)} %add.165), channel_id=1, source_target_pairs={{0,32},{4,36},{8,40},{12,44},{16,48},{20,52},{24,56},{28,60},{32,0... | collective-permute-start | bytes 1966088 | tf_op jit(solution)/shard_map/ppermute | solution.py:14
  448.2 24.1 %copy-start.13 = (f32[128,1280]{1,0:T(8,128)S(1)}, f32[128,1280]{1,0:T(8,128)}, u32[]{:S(2)}) copy-start(f32[128,1280]{1,0:T(8,128)} %copy-done.12) | copy-start | bytes 1966084
  448.2 91.6 %collective-permute-start.10 = (f32[2,128,1280]{2,1,0:T(8,128)S(1)}, f32[2,128,1280]{2,1,0:T(8,128)S(1)}, u32[]{:S(2)}, u32[]{:S(2)}) collective-permute-start(f32[2,128,1280]{2,1,0:T(8,128)S(1)} %slice_add_fusion.3), channel_id=1, source_target_pairs={{0,64},{4,68},{8,72},{12,76},{16,80},{20,84},{24,88},{28,92},{32,9... | collective-permute-start | bytes 3932168 | tf_op jit(solution)/shard_map/ppermute | solution.py:14
  472.2 61.5 %collective-permute-start.4 = (f32[128,1280]{1,0:T(8,128)S(1)}, f32[128,1280]{1,0:T(8,128)S(1)}, u32[]{:S(2)}, u32[]{:S(2)}) collective-permute-start(f32[128,1280]{1,0:T(8,128)S(1)} %add.166), channel_id=1, source_target_pairs={{0,64},{4,68},{8,72},{12,76},{16,80},{20,84},{24,88},{28,92},{32,9... | collective-permute-start | bytes 1966088 | tf_op jit(solution)/shard_map/ppermute | solution.py:14
  533.7 42.7 %collective-permute-start.5 = (f32[128,1280]{1,0:T(8,128)S(1)}, f32[128,1280]{1,0:T(8,128)S(1)}, u32[]{:S(2)}, u32[]{:S(2)}) collective-permute-start(f32[128,1280]{1,0:T(8,128)S(1)} %add.167), channel_id=1, source_target_pairs={{0,128},{4,132},{8,136},{12,140},{16,144},{20,148},{24,152},{28,15... | collective-permute-start | bytes 1966088 | tf_op jit(solution)/shard_map/ppermute | solution.py:14
  539.9 54.4 %collective-permute-start.11 = (f32[1,128,1280]{2,1,0:T(8,128)S(1)}, f32[1,128,1280]{2,1,0:T(8,128)S(1)}, u32[]{:S(2)}, u32[]{:S(2)}) collective-permute-start(f32[1,128,1280]{2,1,0:T(8,128)S(1)} %slice_add_fusion.4), channel_id=1, source_target_pairs={{0,128},{4,132},{8,136},{12,140},{16,144},{20,148},{24,152},{28,15... | collective-permute-start | bytes 1966088 | tf_op jit(solution)/shard_map/ppermute | solution.py:14
  622.8 3.0 copy-start.9
  627.0 3.2 copy-start.6
  (17 other events, 30.7 us)
Sparse Core Ops, SparseCore 0:
  627.1 77.3 all-reduce.1
where the time goes:
time: 717 us; the launch traced here: 713 us
  waiting for transfers between devices  350 us (49%)
  local copies, waits for them, and re-layouts  184 us (26%)
  matrix products  80 us (11%)
  other arithmetic  66.8 us (9%)
  starting transfers between devices  17.5 us (2%)
  between operations  14.3 us (2%)
    ppermute x12, waiting for transfers between devices, partner_2(): return lax.ppermute(value, axis, pairs)  278 us
    psum x1, waiting for transfers between devices, local(): grad_qk = lax.psum(head_part, 'head')  72.3 us
    dynamic_update_slice x20, local copies, waits for them, and re-layouts, head_pair(): lax.dynamic_update_slice_in_dim(inner_out, part_out, col_start, 1)  35 us
    reshape x10, local copies, waits for them, and re-layouts, head_pair(): weight = jnp.broadcast_to(pair_weight[:, :, None, :, None], (2, span_coun...  34.2 us
    dynamic_slice x20, local copies, waits for them, and re-layouts, head_pair(): lax.dynamic_slice_in_dim(cotangent, col_start, pair_cols, 1)  32.4 us
    broadcast_in_dim x10, local copies, waits for them, and re-layouts, head_pair(): jnp.broadcast_to(pair_weight[:, :, None, :, None], (2, span_count, CH, sp...  24 us
    add x10, other arithmetic, head_pair(): d_score = d_score + jnp.sum(jnp.where(causal, weight * d_mix, 0.0), axis=0)  23.9 us
    ppermute x12, starting transfers between devices, partner_2(): return lax.ppermute(value, axis, pairs)  17.5 us
  transfers between devices with their start and end apart: 13, of which 9 were waited for; matrix products, arithmetic and copies ran while one was open for 36% of the time, Pallas kernels for 0%

commit v1 on v0

--- a/solution.py
+++ b/solution.py
@@ -130,7 +130,7 @@
         d_score, q_float, (((0,), (0,)), ((), ())), precision=precise
     )
     head_part = dq_inner + dq_outer + dk_outer
-    grad_qk = lax.psum(head_part, "head")
+    grad_qk = jnp.sum(lax.all_gather(head_part, "head"), axis=0)
     grad_values = (dv_inner + dv_outer).astype(jnp.bfloat16)
     return (mixed, grad_qk, grad_values)
 

time: 717 us -> 695 us (0.969)
  waiting for transfers between devices: 350 us -> 326 us
    psum x1 -> x0, waiting for transfers between devices: 72.3 us -> none  [local(): grad_qk = lax.psum(head_part, 'head')]
    all_gather x0 -> x1, waiting for transfers between devices: none -> 48.3 us  [local(): grad_qk = jnp.sum(lax.all_gather(head_part, 'head'), axis=0)]
  transfers between devices with their start and end apart: 13 -> 13, of which waited for: 9 -> 9; matrix products, arithmetic and copies ran while one was open for 36% -> 37% of each run, Pallas kernels for 0% -> 0%
where the time goes in v1:
time: 695 us; the launch traced here: 691 us
  waiting for transfers between devices  326 us (47%)
  local copies, waits for them, and re-layouts  184 us (26%)
  matrix products  81.4 us (12%)
  other arithmetic  67 us (10%)
  starting transfers between devices  17.5 us (3%)
  between operations  14.3 us (2%)
    ppermute x12, waiting for transfers between devices, partner_2(): return lax.ppermute(value, axis, pairs)  278 us
    all_gather x1, waiting for transfers between devices, local(): grad_qk = jnp.sum(lax.all_gather(head_part, 'head'), axis=0)  48.3 us
    dynamic_update_slice x20, local copies, waits for them, and re-layouts, head_pair(): lax.dynamic_update_slice_in_dim(inner_out, part_out, col_start, 1)  35 us
    reshape x10, local copies, waits for them, and re-layouts, head_pair(): weight = jnp.broadcast_to(pair_weight[:, :, None, :, None], (2, span_coun...  34.2 us
    dynamic_slice x20, local copies, waits for them, and re-layouts, head_pair(): lax.dynamic_slice_in_dim(cotangent, col_start, pair_cols, 1)  32.4 us
    broadcast_in_dim x10, local copies, waits for them, and re-layouts, head_pair(): jnp.broadcast_to(pair_weight[:, :, None, :, None], (2, span_count, CH, sp...  24 us
    add x10, other arithmetic, head_pair(): d_score = d_score + jnp.sum(jnp.where(causal, weight * d_mix, 0.0), axis=0)  23.9 us
    ppermute x12, starting transfers between devices, partner_2(): return lax.ppermute(value, axis, pairs)  17.5 us
  transfers between devices with their start and end apart: 13, of which 9 were waited for; matrix products, arithmetic and copies ran while one was open for 37% of the time, Pallas kernels for 0%

profile of v1, /device:TPU:2, one launch (start us, length us, event | category | flops | bytes accessed | tf_op | source)
XLA Modules:
  0.0 691.2 jit_solution(17752920025509780937)
XLA Ops:
  8.1 4.5 fusion.36
  12.6 6.3 copy.78
  19.9 2.7 copy-done.2
  24.0 10.3 %fusion.37 = f32[1280,6,128]{2,1,0:T(8,128)} fusion(f32[8,6,1280]{0,1,2:T(8,128)S(1)} %bitcast.109, f32[8,128,1280]{1,0,2:T(8,128)S(1)} %copy-done.4), kind=kOutput, calls=%fused_computation.70 | convolution fusion | flops 94371840 | bytes 9420800 | tf_op jit(solution)/shard_map/cij,clj->lij/dot_general | solution.py:52
  34.3 5.7 copy.79
  39.9 7.0 %collective-permute-done.6 = f32[6,128,1280]{2,1,0:T(8,128)S(1)} collective-permute-done((f32[6,128,1280]{2,1,0:T(8,128)}, f32[6,128,1280]{2,1,0:T(8,128)S(1)}, u32[]{:S(2)}, u32[]{:S(2)}) %collective-permute-start.6) | collective-permute-done | bytes 3932192 | tf_op jit(solution)/shard_map/ppermute | solution.py:14
  46.9 3.8 slice_add_fusion
  53.1 71.2 %collective-permute-done.7 = f32[5,128,1280]{2,1,0:T(8,128)S(1)} collective-permute-done((f32[5,128,1280]{2,1,0:T(8,128)S(1)}, f32[5,128,1280]{2,1,0:T(8,128)S(1)}, u32[]{:S(2)}, u32[]{:S(2)}) %collective-permute-start.7) | collective-permute-done | bytes 3276832 | tf_op jit(solution)/shard_map/ppermute | solution.py:14
  135.8 64.5 %collective-permute-done.1 = f32[128,1280]{1,0:T(8,128)S(1)} collective-permute-done((f32[128,1280]{1,0:T(8,128)S(1)}, f32[128,1280]{1,0:T(8,128)S(1)}, u32[]{:S(2)}, u32[]{:S(2)}) %collective-permute-start.1) | collective-permute-done | bytes 655392 | tf_op jit(solution)/shard_map/ppermute | solution.py:14
  202.9 3.7 slice_add_fusion.2
  210.3 230.8 %while.19 = (s32[]{:T(128)}, f32[512,1280]{1,0:T(8,128)}, f32[512,1280]{0,1:T(8,128)}, f32[512,512]{1,0:T(8,128)}, bf16[512,1280]{1,0:T(8,128)(2,1)S(1)}, /*inde...) while((s32[]{:T(128)}, f32[512,1280]{1,0:T(8,128)}, ...), condition=%wide.region_2.3_spmd.clone.clone, body=%wide.region_0.2_spmd.clone.clone.sunk | while | flops 204996608 | bytes 29099832 | solution.py:116
  215.8 3.4 reshape.142
  238.0 3.4 reshape.142
  261.2 3.4 reshape.142
  284.3 3.4 reshape.142
  307.5 3.4 reshape.142
  330.8 3.4 reshape.142
  353.9 3.4 reshape.142
  377.1 3.4 reshape.142
  400.3 3.4 reshape.142
  423.4 3.4 reshape.142
  450.7 21.2 %collective-permute-done.3 = f32[128,1280]{1,0:T(8,128)S(1)} collective-permute-done((f32[128,1280]{1,0:T(8,128)S(1)}, f32[128,1280]{1,0:T(8,128)S(1)}, u32[]{:S(2)}, u32[]{:S(2)}) %collective-permute-start.3) | collective-permute-done | bytes 655392 | tf_op jit(solution)/shard_map/ppermute | solution.py:14
  474.0 59.5 %collective-permute-done.4 = f32[128,1280]{1,0:T(8,128)S(1)} collective-permute-done((f32[128,1280]{1,0:T(8,128)S(1)}, f32[128,1280]{1,0:T(8,128)S(1)}, u32[]{:S(2)}, u32[]{:S(2)}) %collective-permute-start.4) | collective-permute-done | bytes 655392 | tf_op jit(solution)/shard_map/ppermute | solution.py:14
  533.6 6.0 collective-permute-start.5
  541.8 34.5 %collective-permute-done.5 = f32[128,1280]{1,0:T(8,128)S(1)} collective-permute-done((f32[128,1280]{1,0:T(8,128)S(1)}, f32[128,1280]{1,0:T(8,128)S(1)}, u32[]{:S(2)}, u32[]{:S(2)}) %collective-permute-start.5) | collective-permute-done | bytes 655392 | tf_op jit(solution)/shard_map/ppermute | solution.py:14
  576.3 17.7 %collective-permute-done.11 = f32[1,128,1280]{2,1,0:T(8,128)S(1)} collective-permute-done((f32[1,128,1280]{2,1,0:T(8,128)S(1)}, f32[1,128,1280]{2,1,0:T(8,128)S(1)}, u32[]{:S(2)}, u32[]{:S(2)}) %collective-permute-start.11) | collective-permute-done | bytes 655392 | tf_op jit(solution)/shard_map/ppermute | solution.py:14
  594.1 3.0 fusion.9
  597.0 5.7 copy.73
  602.8 13.7 %convert_bitcast_fusion = bf16[8,128,1280]{1,0,2:T(8,128)(2,1)} fusion(f32[6,128,1280]{1,0,2:T(8,128)} %copy.73, f32[8,6,1280]{0,1,2:T(8,128)} %bitcast.110), kind=kOutput, calls=%fused_computation.17 | convolution fusion | flops 95682560 | bytes 6799360 | tf_op jit(solution)/shard_map/clj,lij->cij/dot_general | solution.py:68
  616.5 3.8 copy.75
  625.1 3.3 fusion.3
  634.0 48.3 %all-gather.3.cloned.1.call-done = f32[2048,128]{1,0:T(8,128)} async-done(((f32[512,128]{1,0:T(8,128)}), f32[2048,128]{1,0:T(8,128)}) %all-gather.3.cloned.1.call-update) | async-done | bytes 1048592 | tf_op jit(solution)/shard_map/all_gather | solution.py:133
  (264 shorter events, 245.5 us)
Async XLA Ops:
  7.2 675.1 %all-gather.3.cloned.1.call-start = ((), (), s32[]{:S(2)}) async-start(), calls=%async_computation | async-start | bytes 1310720 | tf_op jit(solution)/shard_map/all_gather | solution.py:133
  12.6 6.3 copy-start.15
  12.6 6.6 copy-start.16
  19.6 4.4 copy-start.4
  19.9 2.7 copy-start.2
  39.9 7.0 %collective-permute-start.6 = (f32[6,128,1280]{2,1,0:T(8,128)}, f32[6,128,1280]{2,1,0:T(8,128)S(1)}, u32[]{:S(2)}, u32[]{:S(2)}) collective-permute-start(f32[6,128,1280]{2,1,0:T(8,128)} %bitcast.117), channel_id=1, source_target_pairs={{0,4},{4,0},{8,12},{12,8},{16,20},{20,16},{24,28},{28,24},{32,36},... | collective-permute-start | bytes 11796488 | tf_op jit(solution)/shard_map/ppermute | solution.py:14
  46.9 3.8 copy-start.9
  50.7 77.8 %copy-start.6 = (bf16[512,1280]{1,0:T(8,128)(2,1)S(1)}, bf16[512,1280]{1,0:T(8,128)(2,1)}, u32[]{:S(2)}) copy-start(bf16[512,1280]{1,0:T(8,128)(2,1)} %param.8) | copy-start | bytes 3932164
  50.7 73.6 %collective-permute-start.7 = (f32[5,128,1280]{2,1,0:T(8,128)S(1)}, f32[5,128,1280]{2,1,0:T(8,128)S(1)}, u32[]{:S(2)}, u32[]{:S(2)}) collective-permute-start(f32[5,128,1280]{2,1,0:T(8,128)S(1)} %slice_add_fusion), channel_id=1, source_target_pairs={{0,8},{4,12},{8,0},{12,4},{16,24},{20,28},{24,16},{28,20},{32,40},... | collective-permute-start | bytes 9830408 | tf_op jit(solution)/shard_map/ppermute | solution.py:14
  124.3 2.6 copy-start.10
  126.9 76.0 %collective-permute-start.8 = (f32[4,128,1280]{2,1,0:T(8,128)}, f32[4,128,1280]{2,1,0:T(8,128)}, u32[]{:S(2)}, u32[]{:S(2)}) collective-permute-start(f32[4,128,1280]{2,1,0:T(8,128)} %slice_add_fusion.1), channel_id=1, source_target_pairs={{0,16},{4,20},{8,24},{12,28},{16,0},{20,4},{24,8},{28,12},{32,48},... | collective-permute-start | bytes 7864328 | tf_op jit(solution)/shard_map/ppermute | solution.py:14
  128.9 2.2 collective-permute-start
  132.0 68.3 %collective-permute-start.1 = (f32[128,1280]{1,0:T(8,128)S(1)}, f32[128,1280]{1,0:T(8,128)S(1)}, u32[]{:S(2)}, u32[]{:S(2)}) collective-permute-start(f32[128,1280]{1,0:T(8,128)S(1)} %add.161), channel_id=1, source_target_pairs={{0,8},{4,12},{8,0},{12,4},{16,24},{20,28},{24,16},{28,20},{32,40},... | collective-permute-start | bytes 1966088 | tf_op jit(solution)/shard_map/ppermute | solution.py:14
  200.2 6.4 copy-start.11
  201.3 241.7 %collective-permute-start.2 = (f32[128,1280]{1,0:T(8,128)}, f32[128,1280]{1,0:T(8,128)}, u32[]{:S(2)}, u32[]{:S(2)}) collective-permute-start(f32[128,1280]{1,0:T(8,128)} %add.162), channel_id=1, source_target_pairs={{0,16},{4,20},{8,24},{12,28},{16,0},{20,4},{24,8},{28,12},{32,48},... | collective-permute-start | bytes 1966088 | tf_op jit(solution)/shard_map/ppermute | solution.py:14
  206.6 239.6 %collective-permute-start.9 = (f32[3,128,1280]{2,1,0:T(8,128)}, f32[3,128,1280]{2,1,0:T(8,128)}, u32[]{:S(2)}, u32[]{:S(2)}) collective-permute-start(f32[3,128,1280]{2,1,0:T(8,128)} %slice_add_fusion.2), channel_id=1, source_target_pairs={{0,32},{4,36},{8,40},{12,44},{16,48},{20,52},{24,56},{28,60},{32,0... | collective-permute-start | bytes 5898248 | tf_op jit(solution)/shard_map/ppermute | solution.py:14
  253.2 2.5 copy-start.7
  276.3 2.5 copy-start.7
  299.6 2.5 copy-start.7
  322.8 2.5 copy-start.7
  345.9 2.5 copy-start.7
  369.1 2.5 copy-start.7
  392.3 2.5 copy-start.7
  415.4 2.5 copy-start.7
  442.9 6.9 copy-start.14
  444.4 27.6 %collective-permute-start.3 = (f32[128,1280]{1,0:T(8,128)S(1)}, f32[128,1280]{1,0:T(8,128)S(1)}, u32[]{:S(2)}, u32[]{:S(2)}) collective-permute-start(f32[128,1280]{1,0:T(8,128)S(1)} %add.163), channel_id=1, source_target_pairs={{0,32},{4,36},{8,40},{12,44},{16,48},{20,52},{24,56},{28,60},{32,0... | collective-permute-start | bytes 1966088 | tf_op jit(solution)/shard_map/ppermute | solution.py:14
  448.1 24.1 %copy-start.12 = (f32[128,1280]{1,0:T(8,128)S(1)}, f32[128,1280]{1,0:T(8,128)}, u32[]{:S(2)}) copy-start(f32[128,1280]{1,0:T(8,128)} %copy-done.11) | copy-start | bytes 1966084
  448.1 91.6 %collective-permute-start.10 = (f32[2,128,1280]{2,1,0:T(8,128)S(1)}, f32[2,128,1280]{2,1,0:T(8,128)S(1)}, u32[]{:S(2)}, u32[]{:S(2)}) collective-permute-start(f32[2,128,1280]{2,1,0:T(8,128)S(1)} %slice_add_fusion.3), channel_id=1, source_target_pairs={{0,64},{4,68},{8,72},{12,76},{16,80},{20,84},{24,88},{28,92},{32,9... | collective-permute-start | bytes 3932168 | tf_op jit(solution)/shard_map/ppermute | solution.py:14
  472.1 61.5 %collective-permute-start.4 = (f32[128,1280]{1,0:T(8,128)S(1)}, f32[128,1280]{1,0:T(8,128)S(1)}, u32[]{:S(2)}, u32[]{:S(2)}) collective-permute-start(f32[128,1280]{1,0:T(8,128)S(1)} %add.164), channel_id=1, source_target_pairs={{0,64},{4,68},{8,72},{12,76},{16,80},{20,84},{24,88},{28,92},{32,9... | collective-permute-start | bytes 1966088 | tf_op jit(solution)/shard_map/ppermute | solution.py:14
  533.6 42.7 %collective-permute-start.5 = (f32[128,1280]{1,0:T(8,128)S(1)}, f32[128,1280]{1,0:T(8,128)S(1)}, u32[]{:S(2)}, u32[]{:S(2)}) collective-permute-start(f32[128,1280]{1,0:T(8,128)S(1)} %add.165), channel_id=1, source_target_pairs={{0,128},{4,132},{8,136},{12,140},{16,144},{20,148},{24,152},{28,15... | collective-permute-start | bytes 1966088 | tf_op jit(solution)/shard_map/ppermute | solution.py:14
  539.7 54.4 %collective-permute-start.11 = (f32[1,128,1280]{2,1,0:T(8,128)S(1)}, f32[1,128,1280]{2,1,0:T(8,128)S(1)}, u32[]{:S(2)}, u32[]{:S(2)}) collective-permute-start(f32[1,128,1280]{2,1,0:T(8,128)S(1)} %slice_add_fusion.4), channel_id=1, source_target_pairs={{0,128},{4,132},{8,136},{12,140},{16,144},{20,148},{24,152},{28,15... | collective-permute-start | bytes 1966088 | tf_op jit(solution)/shard_map/ppermute | solution.py:14
  620.3 3.5 copy-start.8
  (16 other events, 28.1 us)
Sparse Core Ops, SparseCore 0:
  625.2 57.0 all-gather.2
